TPU v7x, 32 devices: a whole 2x2x4 slice. The times are simulated.
32 devices in a mesh: groups: 2 (over y), expert: 4 (over z), dp: 4 (over x, core).
Axes of the slice: x: 2, y: 2, z: 4, core: 2. Of those that a mesh axis runs over, the one named last changes fastest.
Arguments:
- tokens: bfloat16 [4096, 1024], P(('groups', 'expert', 'dp')), parts along dimension 0, may hold values from -6 to 6
- cotangent: bfloat16 [4096, 1024], P(('groups', 'expert', 'dp')), parts along dimension 0, may hold values from -6 to 6
- expert_ids: int32 [4096, 2], P(('groups', 'expert', 'dp')), parts along dimension 0, may hold values from 0 to 3, all different within a row; in each aligned block of 128 rows (0 to 127, 128 to 255, ...) at most 80 rows name the same one
- gates: bfloat16 [4096, 2], P(('groups', 'expert', 'dp')), parts along dimension 0, may hold values from 0.049804688 to 1
- expert_in: bfloat16 [4, 1024, 2048], P('expert', None, 'dp'), may hold values from -0.1875 to 0.1875
- expert_out: bfloat16 [4, 2048, 1024], P('expert', 'dp'), may hold values from -0.125 to 0.125
Outputs:
- grad_tokens: bfloat16 [4096, 1024], P(('groups', 'expert', 'dp')), parts along dimension 0
- grad_gates: bfloat16 [4096, 2], P(('groups', 'expert', 'dp')), parts along dimension 0
- grad_in: bfloat16 [8, 1024, 2048], P(('groups', 'expert'), None, 'dp'), parts along dimension 0
- grad_out: bfloat16 [8, 2048, 1024], P(('groups', 'expert'), 'dp'), parts along dimension 0
There are 2 independent parts, one for each index of `groups`. A program takes and returns all parts, laid end to end along the dimension named above; an argument that names none is the same for every part. Nothing has to cross between parts.
Inputs may be any that keep to these rules, and one draw needn't show every extreme that they name: `expert_ids`: the 2 experts of a token differ. Among the tokens of one device, at most 80 assignments name any one expert, and in every draw some device's tokens name some expert exactly 80 times.
All inputs are finite; a program needn't handle non-finite values.
Results may differ from a plain program's by a relative error of at most 0.0059.
Values may be sent and summed in bfloat16 or wider, within the bound.
A program may use at most 64 MiB of HBM per device.

v0:
```python
import jax
import jax.numpy as jnp
from jax import lax
from jax.sharding import PartitionSpec as P


def expert_rows(pieces, weight_in, weight_out):
    rows_x, rows_g, rows_p = pieces
    pre_act = jnp.dot(rows_x, weight_in, preferred_element_type=jnp.float32)
    activated, pullback = jax.vjp(jax.nn.gelu, pre_act)
    grad_act = jnp.einsum("rd,fd->rf", rows_g, weight_out, preferred_element_type=jnp.float32)
    gate_part = jnp.sum(activated * grad_act, axis=1)
    gate_scale = rows_p.astype(jnp.float32)[:, None]
    hidden_grad = pullback(gate_scale * grad_act)[0].astype(jnp.bfloat16)
    scaled_act = (gate_scale * activated).astype(jnp.bfloat16)
    return (hidden_grad, scaled_act, gate_part)


def per_device(tokens, cotangent, expert_ids, gates, expert_in, expert_out):
    tok_count, width = tokens.shape
    exp_count = lax.axis_size("expert")
    capacity = (5 * tok_count + 2 * exp_count - 1) // (2 * exp_count)
    slot_count = exp_count * capacity
    flat_ids = expert_ids.reshape(2 * tok_count)
    onehot = (flat_ids[:, None] == jnp.arange(exp_count, dtype=jnp.int32)[None, :]).astype(
        jnp.int32
    )
    rank = jnp.sum((jnp.cumsum(onehot, axis=0) - onehot) * onehot, axis=1)
    slot_of = flat_ids * capacity + rank
    placed = jnp.arange(slot_count, dtype=jnp.int32)[:, None] == slot_of[None, :]
    placed_tok = jnp.logical_or(placed[:, 0::2], placed[:, 1::2]).astype(jnp.bfloat16)
    send_x = jnp.dot(placed_tok, tokens, preferred_element_type=jnp.float32).astype(jnp.bfloat16)
    send_g = jnp.dot(placed_tok, cotangent, preferred_element_type=jnp.float32).astype(jnp.bfloat16)
    flat_gates = gates.reshape(2 * tok_count).astype(jnp.float32)
    send_p = jnp.sum(jnp.where(placed, flat_gates[None, :], 0.0), axis=1).astype(jnp.bfloat16)
    recv_x, recv_g, recv_p = (
        lax.all_to_all(
            send_x.reshape(exp_count, capacity, width),
            "expert",
            split_axis=0,
            concat_axis=0,
            tiled=True,
        ),
        lax.all_to_all(
            send_g.reshape(exp_count, capacity, width),
            "expert",
            split_axis=0,
            concat_axis=0,
            tiled=True,
        ),
        lax.all_to_all(
            send_p.reshape(exp_count, capacity), "expert", split_axis=0, concat_axis=0, tiled=True
        ),
    )
    recv_x = recv_x.reshape(slot_count, width)
    recv_g = recv_g.reshape(slot_count, width)
    recv_p = recv_p.reshape(slot_count)
    weight_in = expert_in[0]
    weight_out = expert_out[0]
    pieces = (
        lax.all_gather(recv_x, "dp", axis=0, tiled=True),
        lax.all_gather(recv_g, "dp", axis=0, tiled=True),
        lax.all_gather(recv_p, "dp", axis=0, tiled=True),
    )
    hidden_grad, scaled_act, gate_part = expert_rows(pieces, weight_in, weight_out)
    grad_first = jnp.einsum("rd,rf->df", pieces[0], hidden_grad, preferred_element_type=jnp.float32)
    grad_second = jnp.einsum("rf,rd->fd", scaled_act, pieces[1], preferred_element_type=jnp.float32)
    hidden_all = hidden_grad
    gate_all = gate_part
    grad_first, grad_second, hidden_all, gate_all = (grad_first, grad_second, hidden_all, gate_all)
    hidden_own = lax.all_to_all(hidden_all, "dp", split_axis=0, concat_axis=1, tiled=True)
    gate_own = lax.psum_scatter(gate_all, "dp", scatter_dimension=0, tiled=True)
    input_grad = jnp.einsum(
        "sf,df->sd",
        hidden_own,
        lax.all_gather(weight_in, "dp", axis=1, tiled=True),
        preferred_element_type=jnp.float32,
    )
    back_x, back_p = (
        lax.all_to_all(
            input_grad.astype(jnp.bfloat16).reshape(exp_count, capacity, width),
            "expert",
            split_axis=0,
            concat_axis=0,
            tiled=True,
        ),
        lax.all_to_all(
            gate_own.astype(jnp.bfloat16).reshape(exp_count, capacity),
            "expert",
            split_axis=0,
            concat_axis=0,
            tiled=True,
        ),
    )
    grad_tokens = jnp.dot(
        placed_tok.T, back_x.reshape(slot_count, width), preferred_element_type=jnp.float32
    ).astype(jnp.bfloat16)
    gate_values = back_p.reshape(slot_count).astype(jnp.float32)
    grad_gates = (
        jnp.sum(jnp.where(placed, gate_values[:, None], 0.0), axis=0)
        .reshape(tok_count, 2)
        .astype(jnp.bfloat16)
    )
    return (
        grad_tokens,
        grad_gates,
        grad_first.astype(jnp.bfloat16)[None],
        grad_second.astype(jnp.bfloat16)[None],
    )


def solution(mesh):
    return jax.shard_map(
        per_device,
        mesh=mesh,
        in_specs=(
            P(("groups", "expert", "dp"), None),
            P(("groups", "expert", "dp"), None),
            P(("groups", "expert", "dp"), None),
            P(("groups", "expert", "dp"), None),
            P("expert", None, "dp"),
            P("expert", "dp", None),
        ),
        out_specs=(
            P(("groups", "expert", "dp"), None),
            P(("groups", "expert", "dp"), None),
            P(("groups", "expert"), None, "dp"),
            P(("groups", "expert"), "dp", None),
        ),
        check_vma=False,
    )
```

profile of v0, /device:TPU:0, one launch (start us, length us, event | category | flops | bytes accessed | tf_op | source)
XLA Modules:
  0.0 197.2 jit_solution(2840724695863710383)
XLA Ops:
  7.2 0.9 copy.28
  8.4 1.2 reduce-window.6
  10.1 5.6 %slice.14 = pred[320,128]{1,0:T(8,128)(4,1)S(1)} slice(pred[320,256]{1,0:T(8,128)(4,1)S(1)} %iota_compare_fusion), slice={[0:320:1], [0:256:2]} | slice | bytes 81920 | tf_op jit(solution)/shard_map/slice | solution.py:31
  15.7 5.6 %slice.15 = pred[320,128]{1,0:T(8,128)(4,1)S(1)} slice(pred[320,256]{1,0:T(8,128)(4,1)S(1)} %iota_compare_fusion), slice={[0:320:1], [1:256:2]} | slice | bytes 81920 | tf_op jit(solution)/shard_map/slice | solution.py:31
  21.4 1.3 convolution_convert_fusion.2
  22.6 23.5 %all_to_all.50 = bf16[4,80,1024]{2,1,0:T(8,128)(2,1)} all-to-all(bf16[4,80,1024]{2,1,0:T(8,128)(2,1)S(1)} %bitcast.65), channel_id=1, replica_groups=mesh['groups'=2,'expert'=4,'dp'=4] {'expert'}, dimensions={0} | all-to-all | bytes 1310720 | tf_op jit(solution)/shard_map/all_to_all | solution.py:37
  46.6 19.5 %all_to_all.51 = bf16[4,80,1024]{2,1,0:T(8,128)(2,1)} all-to-all(bf16[4,80,1024]{2,1,0:T(8,128)(2,1)S(1)} %bitcast.66), channel_id=1, replica_groups=mesh['groups'=2,'expert'=4,'dp'=4] {'expert'}, dimensions={0} | all-to-all | bytes 1310720 | tf_op jit(solution)/shard_map/all_to_all | solution.py:44
  66.2 0.7 all-gather.9.cloned.1.call-update
  66.9 0.6 fusion.26
  68.1 2.9 %all-gather.7.cloned.1.call-done = bf16[1280,1024]{1,0:T(8,128)(2,1)} async-done(((bf16[320,1024]{1,0:T(8,128)(2,1)}), bf16[1280,1024]{1,0:T(8,128)(2,1)}) %all-gather.7.cloned.1.call-update) | async-done | bytes 2621456 | tf_op jit(solution)/shard_map/all_gather | solution.py:61
  71.0 4.7 %fusion.15 = f32[1280,512]{1,0:T(8,128)} fusion(bf16[1280,1024]{1,0:T(8,128)(2,1)} %all-gather.7.cloned.1.call-done, bf16[1,1024,512]{2,1,0:T(8,128)(2,1)S(1)} %copy-done.3), kind=kOutput, calls=%fused_computation.23 | convolution fusion | flops 1342177280 | bytes 6291456 | tf_op jit(solution)/shard_map/dot_general | solution.py:9
  75.7 22.4 %all-gather.5.cloned.1.call-done = bf16[1280,1024]{1,0:T(8,128)(2,1)} async-done(((bf16[320,1024]{1,0:T(8,128)(2,1)}), bf16[1280,1024]{1,0:T(8,128)(2,1)}) %all-gather.5.cloned.1.call-update) | async-done | bytes 2621456 | tf_op jit(solution)/shard_map/all_gather | solution.py:62
  98.2 6.2 %multiply_reduce_fusion = (f32[1280]{0:T(1024)S(1)}, f32[1280,512]{1,0:T(8,128)}) fusion(f32[1280,512]{1,0:T(8,128)} %fusion.15, bf16[1280,1024]{1,0:T(8,128)(2,1)} %all-gather.5.cloned.1.call-done, bf16[1,512,1024]{2,1,0:T(8,128)(2,1)S(1)} %copy-done), kind=kOutput, calls=%fused_computation.12 | convolution fusion | flops 1348729600 | bytes 8918016 | tf_op jit(solution)/shard_map/rd,fd->rf/dot_general | solution.py:11
  104.4 6.0 %all-reduce.1 = bf16[1280]{0:T(1024)(128)(2,1)S(1)} all-reduce(f32[1280]{0:T(1024)S(1)} %get-tuple-element.20), channel_id=3, replica_groups=mesh['groups'=2,'expert'=4,'dp'=4] {'dp'}, use_global_device_ids=true, to_apply=%region_5.6.clone | all-reduce | flops 1280 | bytes 7680
  110.5 0.7 all_to_all.43
  111.1 4.7 %all-to-all-start.5 = ((bf16[4,1,80]{2,1,0:T(2,128)(2,1)}), bf16[4,1,80]{2,1,0:T(2,128)(2,1)S(1)}, u32[]{:S(2)}, u32[]{:S(2)}) async-start(bf16[4,1,80]{2,1,0:T(2,128)(2,1)} %all_to_all.43), calls=%async_computation.5 | async-start | bytes 4096 | tf_op jit(solution)/shard_map/all_to_all | solution.py:87
  116.1 5.2 %all-to-all-done.5 = bf16[4,1,80]{2,1,0:T(2,128)(2,1)S(1)} async-done(((bf16[4,1,80]{2,1,0:T(2,128)(2,1)}), bf16[4,1,80]{2,1,0:T(2,128)(2,1)S(1)}, u32[]{:S(2)}, u32[]{:S(2)}) %all-to-all-start.5) | async-done | bytes 672 | tf_op jit(solution)/shard_map/all_to_all | solution.py:87
  121.7 0.7 convert_element_type.100
  122.3 3.2 %all-to-all-start = ((bf16[4,1,80]{2,1,0:T(2,128)(2,1)}), bf16[4,1,80]{2,1,0:T(2,128)(2,1)S(1)}, u32[]{:S(2)}, u32[]{:S(2)}) async-start(bf16[4,1,80]{2,1,0:T(2,128)(2,1)} %convert_element_type.100), calls=%async_computation | async-start | bytes 4096 | tf_op jit(solution)/shard_map/all_to_all | solution.py:51
  126.2 4.8 %all-to-all-done = bf16[4,1,80]{2,1,0:T(2,128)(2,1)S(1)} async-done(((bf16[4,1,80]{2,1,0:T(2,128)(2,1)}), bf16[4,1,80]{2,1,0:T(2,128)(2,1)S(1)}, u32[]{:S(2)}, u32[]{:S(2)}) %all-to-all-start) | async-done | bytes 672 | tf_op jit(solution)/shard_map/all_to_all | solution.py:51
  131.3 5.6 %all-reduce = bf16[1280]{0:T(1024)(128)(2,1)S(1)} all-reduce(bf16[1280]{0:T(1024)(128)(2,1)S(1)} %dynamic-update-slice), channel_id=1, replica_groups=mesh['groups'=2,'expert'=4,'dp'=4] {'dp'}, use_global_device_ids=true, to_apply=%add | all-reduce | flops 1280 | bytes 5120
  137.0 4.7 %fusion.8 = bf16[1280,512]{1,0:T(8,128)(2,1)} fusion(f32[1280,512]{1,0:T(8,128)} %fusion.15, f32[1280,512]{1,0:T(8,128)} %get-tuple-element.21, f32[1280]{0:T(1024)S(1)} %convert_element_type.84), kind=kLoop, calls=%fused_computation.10 | loop fusion | flops 13762560 | bytes 6558720 | tf_op jit(solution)/shard_map/convert_element_type | solution.py:14
  141.7 3.7 %all-to-all-start.3 = ((bf16[4,320,512]{2,1,0:T(8,128)(2,1)}), bf16[4,320,512]{2,1,0:T(8,128)(2,1)S(1)}, u32[]{:S(2)}, u32[]{:S(2)}) async-start(bf16[4,320,512]{2,1,0:T(8,128)(2,1)} %bitcast.61), calls=%async_computation.3 | async-start | bytes 2621440 | tf_op jit(solution)/shard_map/all_to_all | solution.py:71
  145.5 0.6 copy.36
  146.1 16.3 %all-to-all-done.3 = bf16[4,320,512]{2,1,0:T(8,128)(2,1)S(1)} async-done(((bf16[4,320,512]{2,1,0:T(8,128)(2,1)}), bf16[4,320,512]{2,1,0:T(8,128)(2,1)S(1)}, u32[]{:S(2)}, u32[]{:S(2)}) %all-to-all-start.3) | async-done | bytes 1310752 | tf_op jit(solution)/shard_map/all_to_all | solution.py:71
  162.4 1.3 copy.37
  163.7 5.1 %fusion.11 = bf16[320,1024]{1,0:T(8,128)(2,1)} fusion(bf16[320,2048]{1,0:T(8,128)(2,1)} %bitcast.67, bf16[1,1024,2048]{2,1,0:T(8,128)(2,1)} %all-gather.9.cloned.1.call-done), kind=kOutput, calls=%fused_computation.20 | convolution fusion | flops 1342504960 | bytes 6160384 | tf_op jit(solution)/shard_map/sf,df->sd/dot_general | solution.py:73
  168.8 3.5 %all-to-all-start.4 = ((bf16[4,80,1024]{2,1,0:T(8,128)(2,1)}), bf16[4,80,1024]{2,1,0:T(8,128)(2,1)S(1)}, u32[]{:S(2)}, u32[]{:S(2)}) async-start(bf16[4,80,1024]{2,1,0:T(8,128)(2,1)} %bitcast.68), calls=%async_computation.4 | async-start | bytes 1310720 | tf_op jit(solution)/shard_map/all_to_all | solution.py:80
  172.3 4.4 %fusion.9 = bf16[1,1024,512]{2,1,0:T(8,128)(2,1)} fusion(bf16[1280,1024]{1,0:T(8,128)(2,1)} %all-gather.7.cloned.1.call-done, bf16[1280,512]{1,0:T(8,128)(2,1)S(1)} %copy-done.1), kind=kOutput, calls=%fused_computation.16 | convolution fusion | flops 1342701568 | bytes 4980736 | tf_op jit(solution)/shard_map/rd,rf->df/dot_general | solution.py:66
  176.8 2.7 %fusion.10 = bf16[1,512,1024]{2,1,0:T(8,128)(2,1)} fusion(bf16[1280,1024]{1,0:T(8,128)(2,1)S(1)} %copy-done.7, f32[1280]{0:T(1024)S(1)} %convert_element_type.84, f32[1280,512]{1,0:T(8,128)S(1)} %copy-done.2), kind=kOutput, calls=%fused_computation.17 | convolution fusion | flops 1349255168 | bytes 6296576 | tf_op jit(solution)/shard_map/rf,rd->fd/dot_general | solution.py:67
  179.5 10.2 %all-to-all-done.4 = bf16[4,80,1024]{2,1,0:T(8,128)(2,1)S(1)} async-done(((bf16[4,80,1024]{2,1,0:T(8,128)(2,1)}), bf16[4,80,1024]{2,1,0:T(8,128)(2,1)S(1)}, u32[]{:S(2)}, u32[]{:S(2)}) %all-to-all-start.4) | async-done | bytes 655392 | tf_op jit(solution)/shard_map/all_to_all | solution.py:80
  189.7 1.0 convolution_convert_fusion.4
  (48 shorter events, 2.5 us)
Async XLA Ops:
  7.2 91.0 %copy-start = (bf16[1,512,1024]{2,1,0:T(8,128)(2,1)S(1)}, bf16[1,512,1024]{2,1,0:T(8,128)(2,1)}, u32[]{:S(2)}) copy-start(bf16[1,512,1024]{2,1,0:T(8,128)(2,1)} %param.11) | copy-start | bytes 3145732
  7.2 39.1 %copy-start.4 = (bf16[128,1024]{1,0:T(8,128)(2,1)S(1)}, bf16[128,1024]{1,0:T(8,128)(2,1)}, u32[]{:S(2)}) copy-start(bf16[128,1024]{1,0:T(8,128)(2,1)} %param.7) | copy-start | bytes 786436
  7.2 63.8 %all-gather.7.cloned.1.call-start = ((), (), s32[]{:S(2)}) async-start(), calls=%async_computation.7 | async-start | bytes 3276800 | tf_op jit(solution)/shard_map/all_gather | solution.py:61
  46.2 20.7 %copy-start.5 = (u32[32]{0:T(128)S(1)}, u32[32]{0:T(128)}, u32[]{:S(2)}) copy-start(u32[32]{0:T(128)} %constant.26) | copy-start | bytes 388
  46.2 24.8 %copy-start.3 = (bf16[1,1024,512]{2,1,0:T(8,128)(2,1)S(1)}, bf16[1,1024,512]{2,1,0:T(8,128)(2,1)}, u32[]{:S(2)}) copy-start(bf16[1,1024,512]{2,1,0:T(8,128)(2,1)} %param.10) | copy-start | bytes 3145732
  46.2 52.0 %all-gather.5.cloned.1.call-start = ((), (), s32[]{:S(2)}) async-start(), calls=%async_computation.6 | async-start | bytes 3276800 | tf_op jit(solution)/shard_map/all_gather | solution.py:62
  66.1 97.6 %all-gather.9.cloned.1.call-start = ((), (), s32[]{:S(2)}) async-start(), calls=%async_computation.8 | async-start | bytes 5242880 | tf_op jit(solution)/shard_map/all_gather | solution.py:76
  75.7 40.1 %copy-start.6 = (bf16[128,2]{0,1:T(2,128)(2,1)S(1)}, bf16[128,2]{0,1:T(2,128)(2,1)}, u32[]{:S(2)}) copy-start(bf16[128,2]{0,1:T(2,128)(2,1)} %param.9) | copy-start | bytes 1540
  111.1 10.2 %all-to-all-start.5 = ((bf16[4,1,80]{2,1,0:T(2,128)(2,1)}), bf16[4,1,80]{2,1,0:T(2,128)(2,1)S(1)}, u32[]{:S(2)}, u32[]{:S(2)}) async-start(bf16[4,1,80]{2,1,0:T(2,128)(2,1)} %all_to_all.43), calls=%async_computation.5 | async-start | bytes 4096 | tf_op jit(solution)/shard_map/all_to_all | solution.py:87
  122.3 8.7 %all-to-all-start = ((bf16[4,1,80]{2,1,0:T(2,128)(2,1)}), bf16[4,1,80]{2,1,0:T(2,128)(2,1)S(1)}, u32[]{:S(2)}, u32[]{:S(2)}) async-start(bf16[4,1,80]{2,1,0:T(2,128)(2,1)} %convert_element_type.100), calls=%async_computation | async-start | bytes 4096 | tf_op jit(solution)/shard_map/all_to_all | solution.py:51
  141.7 20.8 %all-to-all-start.3 = ((bf16[4,320,512]{2,1,0:T(8,128)(2,1)}), bf16[4,320,512]{2,1,0:T(8,128)(2,1)S(1)}, u32[]{:S(2)}, u32[]{:S(2)}) async-start(bf16[4,320,512]{2,1,0:T(8,128)(2,1)} %bitcast.61), calls=%async_computation.3 | async-start | bytes 2621440 | tf_op jit(solution)/shard_map/all_to_all | solution.py:71
  163.7 8.6 %copy-start.1 = (bf16[1280,512]{1,0:T(8,128)(2,1)S(1)}, bf16[1280,512]{1,0:T(8,128)(2,1)}, u32[]{:S(2)}) copy-start(bf16[1280,512]{1,0:T(8,128)(2,1)} %fusion.8) | copy-start | bytes 3932164
  168.8 20.8 %all-to-all-start.4 = ((bf16[4,80,1024]{2,1,0:T(8,128)(2,1)}), bf16[4,80,1024]{2,1,0:T(8,128)(2,1)S(1)}, u32[]{:S(2)}, u32[]{:S(2)}) async-start(bf16[4,80,1024]{2,1,0:T(8,128)(2,1)} %bitcast.68), calls=%async_computation.4 | async-start | bytes 1310720 | tf_op jit(solution)/shard_map/all_to_all | solution.py:80
  172.3 4.4 %copy-start.2 = (f32[1280,512]{1,0:T(8,128)S(1)}, f32[1280,512]{1,0:T(8,128)}, u32[]{:S(2)}) copy-start(f32[1280,512]{1,0:T(8,128)} %fusion.15) | copy-start | bytes 7864324
  172.3 4.4 %copy-start.7 = (bf16[1280,1024]{1,0:T(8,128)(2,1)S(1)}, bf16[1280,1024]{1,0:T(8,128)(2,1)}, u32[]{:S(2)}) copy-start(bf16[1280,1024]{1,0:T(8,128)(2,1)} %all-gather.5.cloned.1.call-done) | copy-start | bytes 7864324
Sparse Core Ops, SparseCore 0:
  46.3 24.6 all-gather.6
  72.6 25.5 all-gather.4
  99.7 34.5 all-gather.8
where the time goes:
time: 198 us; the launch traced here: 197 us
  waiting for transfers between devices  62.5 us (32%)
  blocking collectives  54.7 us (28%)
  matrix products  25.8 us (13%)
  local copies, waits for them, and re-layouts  17.4 us (9%)
  starting transfers between devices  15.3 us (8%)
  between operations  15.2 us (8%)
  other arithmetic  6.4 us (3%)
    all_to_all x1, blocking collectives, per_device(): lax.all_to_all(send_x.reshape(exp_count, capacity, width), 'expert', spli...  23.5 us
    all_gather x1, waiting for transfers between devices, per_device(): lax.all_gather(recv_g, 'dp', axis=0, tiled=True)  22.4 us
    all_to_all x1, blocking collectives, per_device(): lax.all_to_all(send_g.reshape(exp_count, capacity, width), 'expert', spli...  19.5 us
    all_to_all x1, waiting for transfers between devices, per_device(): lax.all_to_all(hidden_all, 'dp', split_axis=0, concat_axis=1, tiled=True)  16.3 us
    unnamed x2, blocking collectives  11.6 us
    all_to_all x1, waiting for transfers between devices, per_device(): lax.all_to_all(input_grad.astype(jnp.bfloat16).reshape(exp_count, capacit...  10.2 us
    dot_general x1, matrix products, expert_rows(): jnp.einsum('rd,fd->rf', rows_g, weight_out, preferred_element_type=jnp.fl...  6.21 us
    slice x1, local copies, waits for them, and re-layouts, per_device(): placed[:, 0::2]  5.58 us
  transfers between devices with their start and end apart: 7, of which 6 were waited for; matrix products, arithmetic and copies ran while one was open for 14% of the time, Pallas kernels for 0%

commit v1 on v0

v1 whole, which is shorter than its diff:
```python
import functools

import jax
import jax.numpy as jnp
from jax import lax
from jax.experimental import pallas as pl
from jax.experimental.pallas import tpu as pltpu
from jax.sharding import PartitionSpec as P

F32 = jnp.float32
BF16 = jnp.bfloat16


def dot(a, b, ca, cb):
    return lax.dot_general(a, b, (((ca,), (cb,)), ((), ())), preferred_element_type=F32)


def split(v):
    hi = v.astype(BF16)
    return hi, (v - hi.astype(F32)).astype(BF16)


def gelu_both(v):
    k = 0.7978845608028654
    v2 = v * v
    t = jnp.tanh(k * v * (1.0 + 0.044715 * v2))
    half = 0.5 + 0.5 * t
    act = v * half
    slope = half + act * (1.0 - t) * (k * (1.0 + 3.0 * 0.044715 * v2))
    return act, slope


def kernel(
    n_exp, n_dp, cap, width, hid,
    ids_ref, gate_ref, tok_ref, cot_ref, win_hbm, wout_hbm,
    gtok_ref, ggate_ref, gin_ref, gout_ref,
    win, wout, hit_s, rank_s, placed, send, buf, h_buf, a_buf,
    part, sib_in, x_out, x_in, own_sum, z_out, back, g_part, g_in, g_out, g_back,
    w_sem, zs, zr, xs, xr, fs, fr, ps, pr, rs, rr, bs, br, gs, gr, ks, kr,
):
    nx = n_dp // 2
    me = lax.axis_index("expert")
    d = lax.axis_index("dp")
    c = d % 2
    x = d // 2
    tok_count = tok_ref.shape[0]
    lanes = placed.shape[1]
    chunk = n_dp * cap

    def exp_dev(e):
        return {"expert": e}

    def dp_dev(i):
        return {"dp": i}

    sib = x * 2 + (1 - c)

    def x_peer(i):
        return ((x + i) % nx) * 2 + c

    def up(s):
        return (me + s) % n_exp

    def down(s):
        return (me + n_exp - s) % n_exp

    def rows(s, who):
        return pl.ds(pl.multiple_of(s * chunk + who * cap, 16), cap)

    def rcopy(src, dst, ss, rsem, dev):
        return pltpu.make_async_remote_copy(
            src_ref=src, dst_ref=dst, send_sem=ss, recv_sem=rsem,
            device_id=dev, device_id_type=pl.DeviceIdType.MESH,
        )

    cw_in = pltpu.make_async_copy(win_hbm, win, w_sem.at[0])
    cw_out = pltpu.make_async_copy(wout_hbm, wout, w_sem.at[1])
    cw_in.start()
    cw_out.start()

    barrier = pltpu.get_barrier_semaphore()

    for s in range(1, n_exp):
        pl.semaphore_signal(barrier, inc=1, device_id=exp_dev(up(s)), device_id_type=pl.DeviceIdType.MESH)
    for i in range(1, n_dp):
        pl.semaphore_signal(
            barrier, inc=1, device_id=dp_dev((d + i) % n_dp), device_id_type=pl.DeviceIdType.MESH
        )

    ids0 = ids_ref[0:1, :]
    ids1 = ids_ref[1:2, :]
    p0 = gate_ref[0:1, :]
    p1 = gate_ref[1:2, :]
    e_rows = hit_s.shape[0]
    e_iota = lax.broadcasted_iota(jnp.int32, (e_rows, tok_count), 0)
    hit = jnp.where(e_iota == ids0, 1.0, 0.0) + jnp.where(e_iota == ids1, 1.0, 0.0)
    before = jnp.where(
        lax.broadcasted_iota(jnp.int32, (tok_count, tok_count), 0)
        < lax.broadcasted_iota(jnp.int32, (tok_count, tok_count), 1),
        1.0, 0.0,
    )
    rank = dot(hit.astype(BF16), before.astype(BF16), 1, 0)
    slot_iota = lax.broadcasted_iota(jnp.int32, (lanes, tok_count), 0).astype(F32)
    hit_s[...] = hit
    rank_s[...] = rank
    pl.semaphore_wait(barrier, n_exp - 1 + n_dp - 1)

    def z_copy(s, k):
        return rcopy(
            send.at[k, pl.ds(pl.multiple_of(s * cap, 16), cap)], buf.at[k, rows(s, d)],
            zs.at[k, s], zr.at[k, s], exp_dev(up(s)),
        )

    def x_copy(s, k, i):
        return rcopy(
            buf.at[k, rows(s, d)], buf.at[k, rows(s, d)],
            xs.at[k, s, i - 1], xr.at[k, s, i - 1], dp_dev(x_peer(i)),
        )

    def x_landed(s, k, i):
        who = ((x + nx - i) % nx) * 2 + c
        ref = buf.at[k, rows(s, who)]
        return rcopy(ref, ref, xs.at[k, s, i - 1], xr.at[k, s, i - 1], dp_dev(x_peer(i)))

    def f_copy(s, k, i, core):
        ref = buf.at[k, rows(s, ((x + nx - i) % nx) * 2 + core)]
        return rcopy(ref, ref, fs.at[k, s, i], fr.at[k, s, i], dp_dev(sib))

    def fill(s, k):
        e = up(s)
        h_row = hit_s[pl.ds(e, 1), :]
        r_row = rank_s[pl.ds(e, 1), :]
        here = jnp.where(slot_iota == r_row, h_row, 0.0)
        if k == 0:
            placed[pl.ds(pl.multiple_of(s * lanes, 16), lanes), :] = here.astype(BF16)
            return dot(here[:cap].astype(BF16), tok_ref[...], 1, 0).astype(BF16)
        p_row = jnp.where(ids0 == e, p0, p1)
        return dot((here[:cap] * p_row).astype(BF16), cot_ref[...], 1, 0).astype(BF16)

    def start_send(s):
        for k in range(2):
            send[k, pl.ds(pl.multiple_of(s * cap, 16), cap), :] = fill(s, k)
            z_copy(s, k).start()

    def spread(s, k):
        for i in range(1, nx):
            x_copy(s, k, i).start()
        f_copy(s, k, 0, c).start()

    def f1(s):
        for k in range(2):
            z_copy(s, k).wait_recv()
            spread(s, k)

    def f2(s):
        for k in range(2):
            for i in range(1, nx):
                x_landed(s, k, i).wait_recv()
                f_copy(s, k, i, c).start()

    def p_copy(s, i):
        who = ((x + i) % nx) * 2 + (1 - c)
        return rcopy(
            part.at[rows(s, who)], sib_in.at[s, i], ps.at[s, i], pr.at[s, i], dp_dev(sib)
        )

    def compute(s):
        for k in range(2):
            for i in range(nx):
                f_copy(s, k, i, 1 - c).wait_recv()
        here = pl.ds(pl.multiple_of(s * chunk, 16), chunk)
        pre = dot(buf[0, here, :], win[...], 1, 0)
        grad_act = dot(buf[1, here, :], wout[...], 1, 1)
        act, slope = gelu_both(pre)
        hidden = (grad_act * slope).astype(BF16)
        h_buf[here, :] = hidden
        a_buf[here, :] = act.astype(BF16)
        part[here, :] = dot(hidden, win[...], 1, 1).astype(BF16)
        for i in range(nx):
            p_copy(s, i).start()
        hi, lo = split(act * grad_act)
        ones = jnp.ones((8, hid), BF16)
        for i in range(n_dp):
            own = slice(i * cap, (i + 1) * cap)
            g_part[i, s, :, 0:cap] = dot(ones, hi[own], 1, 1) + dot(ones, lo[own], 1, 1)

    def r_copy(s, i):
        return rcopy(
            x_out.at[s, i - 1], x_in.at[s, i - 1], rs.at[s, i - 1], rr.at[s, i - 1], dp_dev(x_peer(i))
        )

    def r1(s):
        for i in list(range(1, nx)) + [0]:
            p_copy(s, i).wait_recv()
            who = ((x + i) % nx) * 2 + c
            total = part[rows(s, who), :].astype(F32) + sib_in[s, i].astype(F32)
            if i == 0:
                own_sum[s] = total
            else:
                x_out[s, i - 1] = total.astype(BF16)
                r_copy(s, i).start()

    def b_copy(s):
        return rcopy(
            z_out.at[s], back.at[pl.ds(pl.multiple_of(s * cap, 16), cap)],
            bs.at[s], br.at[s], exp_dev(down(s)),
        )

    def r2(s):
        total = own_sum[s]
        for i in range(1, nx):
            r_copy(s, i).wait_recv()
            total += x_in[s, i - 1].astype(F32)
        return total.astype(BF16)

    def r2_send(s):
        z_out[s] = r2(s)
        b_copy(s).start()

    def g_copy(i):
        return rcopy(
            g_part.at[(d + i) % n_dp], g_in.at[i - 1], gs.at[i - 1], gr.at[i - 1],
            dp_dev((d + i) % n_dp),
        )

    def k_copy(s):
        return rcopy(g_out.at[s], g_back.at[s], ks.at[s], kr.at[s], exp_dev(down(s)))

    g_part[...] = jnp.zeros_like(g_part)
    unroll = n_exp <= 4

    def over(low, high, body):
        if unroll:
            for s in range(low, high):
                body(s)
        else:
            lax.fori_loop(low, high, lambda s, t: (body(s), t)[1], 0)

    for k in range(2):
        buf[k, rows(0, d), :] = fill(0, k)
        spread(0, k)
    over(1, n_exp, start_send)
    cw_in.wait()
    cw_out.wait()

    f1(1)
    f2(0)
    compute(0)
    f1(2)
    f2(1)
    compute(1)
    r1(0)

    def steady(t):
        f1(t)
        f2(t - 1)
        compute(t - 1)
        r1(t - 2)

        if unroll and t == 3:
            back[0:cap, :] = r2(0)
        else:
            r2_send(t - 3)

    if unroll:
        over(3, n_exp, steady)
    else:
        f1(3)
        f2(2)
        compute(2)
        r1(1)
        back[0:cap, :] = r2(0)
        over(4, n_exp, steady)
    last = n_exp - 1
    f2(last)
    compute(last)
    for i in range(1, n_dp):
        g_copy(i).start()
    r1(last - 1)
    r2_send(last - 2)
    tile = 256

    def in_tile(j, t):
        cols = pl.ds(pl.multiple_of(j * tile, tile), tile)
        gin_ref[cols, :] = dot(buf[0, :, cols], h_buf[...], 0, 0).astype(BF16)
        return t

    def out_tile(j, t):
        cols = pl.ds(pl.multiple_of(j * tile, tile), tile)
        gout_ref[:, cols] = dot(a_buf[...], buf[1, :, cols], 0, 0).astype(BF16)
        return t

    r1(last)
    r2_send(last - 1)
    lax.fori_loop(0, width // tile, in_tile, 0)
    r2_send(last)
    g_sum = g_part[d]
    for i in range(1, n_dp):
        g_copy(i).wait_recv()
        g_sum += g_in[i - 1]
    g_out[...] = g_sum
    over(1, n_exp, lambda s: k_copy(s).start())
    lax.fori_loop(0, width // tile, out_tile, 0)
    g_back[0] = g_out[0]
    over(1, n_exp, lambda s: k_copy(s).wait_recv())
    gate0 = jnp.zeros((8, tok_count), F32)
    gate1 = jnp.zeros((8, tok_count), F32)
    for s in range(n_exp):
        hi, lo = split(g_back[s])
        mine = placed[s * lanes : (s + 1) * lanes, :]
        value = dot(hi, mine, 1, 0) + dot(lo, mine, 1, 0)
        gate0 += jnp.where(ids0 == up(s), value, 0.0)
        gate1 += jnp.where(ids1 == up(s), value, 0.0)
    ggate_ref[0:8, :] = gate0 / p0
    ggate_ref[8:16, :] = gate1 / p1

    over(1, n_exp, lambda s: b_copy(s).wait_recv())
    total = jnp.zeros((tok_count, width), F32)
    for s in range(n_exp):
        total += dot(
            placed[s * lanes : s * lanes + cap, :], back[s * cap : (s + 1) * cap, :], 0, 0
        )
    gtok_ref[...] = total.astype(BF16)

    def drain(s):
        for k in range(2):
            z_copy(s, k).wait_send()
        b_copy(s).wait_send()
        k_copy(s).wait_send()

    def drain_all(s):
        for k in range(2):
            for i in range(1, nx):
                x_copy(s, k, i).wait_send()
            for i in range(nx):
                f_copy(s, k, i, c).wait_send()
        for i in range(nx):
            p_copy(s, i).wait_send()
        for i in range(1, nx):
            r_copy(s, i).wait_send()

    over(1, n_exp, drain)
    over(0, n_exp, drain_all)
    for i in range(1, n_dp):
        g_copy(i).wait_send()


def per_device(tokens, cotangent, expert_ids, gates, expert_in, expert_out):
    tok_count, width = tokens.shape
    n_exp = lax.axis_size("expert")
    n_dp = lax.axis_size("dp")
    nx = n_dp // 2
    hid = expert_in.shape[2]
    cap = (5 * tok_count + 2 * n_exp - 1) // (2 * n_exp)
    cap = (cap + 15) // 16 * 16
    chunk = n_dp * cap
    lanes = 128
    e_rows = (n_exp + 15) // 16 * 16
    vmem = pl.BlockSpec(memory_space=pltpu.VMEM)
    hbm = pl.BlockSpec(memory_space=pl.ANY)
    dma = pltpu.SemaphoreType.DMA
    far = max(nx - 1, 1)
    grad_tokens, gate_rows, grad_in, grad_out = pl.pallas_call(
        functools.partial(kernel, n_exp, n_dp, cap, width, hid),
        out_shape=(
            jax.ShapeDtypeStruct((tok_count, width), BF16),
            jax.ShapeDtypeStruct((16, tok_count), F32),
            jax.ShapeDtypeStruct((width, hid), BF16),
            jax.ShapeDtypeStruct((hid, width), BF16),
        ),
        in_specs=[vmem] * 4 + [hbm] * 2,
        out_specs=(vmem,) * 4,
        scratch_shapes=[
            pltpu.VMEM((width, hid), BF16),
            pltpu.VMEM((hid, width), BF16),
            pltpu.VMEM((e_rows, tok_count), F32),
            pltpu.VMEM((e_rows, tok_count), F32),
            pltpu.VMEM((n_exp * lanes, tok_count), BF16),
            pltpu.VMEM((2, n_exp * cap, width), BF16),
            pltpu.VMEM((2, n_exp * chunk, width), BF16),
            pltpu.VMEM((n_exp * chunk, hid), BF16),
            pltpu.VMEM((n_exp * chunk, hid), BF16),
            pltpu.VMEM((n_exp * chunk, width), BF16),
            pltpu.VMEM((n_exp, nx, cap, width), BF16),
            pltpu.VMEM((n_exp, far, cap, width), BF16),
            pltpu.VMEM((n_exp, far, cap, width), BF16),
            pltpu.VMEM((n_exp, cap, width), F32),
            pltpu.VMEM((n_exp, cap, width), BF16),
            pltpu.VMEM((n_exp * cap, width), BF16),
            pltpu.VMEM((n_dp, n_exp, 8, lanes), F32),
            pltpu.VMEM((n_dp - 1, n_exp, 8, lanes), F32),
            pltpu.VMEM((n_exp, 8, lanes), F32),
            pltpu.VMEM((n_exp, 8, lanes), F32),
            dma((2,)),
            dma((2, n_exp)), dma((2, n_exp)),
            dma((2, n_exp, far)), dma((2, n_exp, far)),
            dma((2, n_exp, nx)), dma((2, n_exp, nx)),
            dma((n_exp, nx)), dma((n_exp, nx)),
            dma((n_exp, far)), dma((n_exp, far)),
            dma((n_exp,)), dma((n_exp,)),
            dma((n_dp - 1,)), dma((n_dp - 1,)),
            dma((n_exp,)), dma((n_exp,)),
        ],
        compiler_params=pltpu.CompilerParams(
            collective_id=0, has_side_effects=True, vmem_limit_bytes=60 * 1024 * 1024
        ),
    )(
        expert_ids.T, gates.T.astype(F32), tokens, cotangent, expert_in[0], expert_out[0]
    )
    grad_gates = gate_rows[0::8].T.astype(BF16)
    return grad_tokens, grad_gates, grad_in[None], grad_out[None]


def solution(mesh):
    rows = P(("groups", "expert", "dp"), None)
    return jax.shard_map(
        per_device,
        mesh=mesh,
        in_specs=(rows, rows, rows, rows, P("expert", None, "dp"), P("expert", "dp", None)),
        out_specs=(
            rows,
            rows,
            P(("groups", "expert"), None, "dp"),
            P(("groups", "expert"), "dp", None),
        ),
        check_vma=False,
    )
```

time: 198 us -> 84.7 us (0.43)
  Pallas kernels: 0 us -> 76.3 us
  waiting for transfers between devices: 62.5 us -> 0 us
  blocking collectives: 54.7 us -> 0 us
  matrix products: 25.8 us -> 0 us
  starting transfers between devices: 15.3 us -> 0 us
  between operations: 15.2 us -> 0.66 us
  local copies, waits for them, and re-layouts: 17.4 us -> 6.86 us
  other arithmetic: 6.4 us -> 0.57 us
    pallas_call x0 -> x1, Pallas kernels: none -> 76.3 us  [per_device(): pl.pallas_call(functools.partial(kernel, n_exp, n_dp, cap, width, hid), o...]
    all_to_all x2 -> x0, blocking collectives: 43.1 us -> none  [the longest x1 23.5 us: per_device(): lax.all_to_all(send_x.reshape(exp_count, capacity, width), 'expert', spli...]
    all_to_all x4 -> x0, waiting for transfers between devices: 36.5 us -> none  [the longest x1 16.3 us: per_device(): lax.all_to_all(hidden_all, 'dp', split_axis=0, concat_axis=1, tiled=True)]
    dot_general x8 -> x0, matrix products: 25.8 us -> none  [the longest x1 6.21 us: expert_rows(): jnp.einsum('rd,fd->rf', rows_g, weight_out, preferred_element_type=jnp.fl...]
    all_gather x3 -> x0, waiting for transfers between devices: 25.3 us -> none  [the longest x1 22.4 us: per_device(): lax.all_gather(recv_g, 'dp', axis=0, tiled=True)]
    all_to_all x4 -> x0, starting transfers between devices: 15.1 us -> none  [the longest x1 4.72 us: per_device(): lax.all_to_all(gate_own.astype(jnp.bfloat16).reshape(exp_count, capacity)...]
    unnamed x2 -> x0, blocking collectives: 11.6 us -> none
    slice x4 -> x1, local copies, waits for them, and re-layouts: 11.3 us -> 0.53 us  [per_device(): grad_gates = gate_rows[0::8].T.astype(BF16)]
  transfers between devices with their start and end apart: 7 -> 0, of which waited for: 6 -> 0; matrix products, arithmetic and copies ran while one was open for 14% -> 0% of each run, Pallas kernels for 0% -> 0%
where the time goes in v1:
time: 84.7 us; the launch traced here: 84.4 us
  Pallas kernels  76.3 us (90%)
  local copies, waits for them, and re-layouts  6.86 us (8%)
    pallas_call x1, Pallas kernels, per_device(): pl.pallas_call(functools.partial(kernel, n_exp, n_dp, cap, width, hid), o...  76.3 us
    unnamed x9, local copies, waits for them, and re-layouts  6.33 us

profile of v1, /device:TPU:0, one launch (start us, length us, event | category | flops | bytes accessed | tf_op | source)
XLA Modules:
  0.0 84.4 jit_solution(6141656414382313373)
XLA Ops:
  0.6 0.0 copy-start.2
  0.6 0.6 copy-done.2
  1.3 0.6 convert_bitcast_fusion.gate_ref
  1.9 76.3 %shard_map.93 = (bf16[128,1024]{1,0:T(8,128)(2,1)}, f32[16,128]{1,0:T(8,128)}, bf16[1024,512]{1,0:T(8,128)(2,1)}, bf16[512,1024]{1,0:T(8,128)(2,1)}) custom-call(s32[2,128]{1,0:T(2,128)} %bitcast.12, f32[2,128]{1,0:T(2,128)} %convert_bitcast_fusion.gate_ref, bf16[128,1024]{1,0:T(8,128)(2,1)} %tok_ref.1, bf16[128,1024]{1,0:T(8,128)(2,1)} %cot_ref.1, ...), custom_call_target="tpu_custom_call" | custom-call | tf_op jit(solution)/shard_map/pallas_call | solution.py:363
  78.2 0.0 copy-start.1
  78.2 0.7 copy-done.1
  78.9 0.5 slice.4
  79.4 1.7 %copy.13 = bf16[128,1024]{1,0:T(8,128)(2,1)} copy(bf16[128,1024]{1,0:T(8,128)(2,1)} %get-tuple-element.16) | data formatting | bytes 524288
  81.1 0.0 copy-start
  81.1 2.4 %copy.14 = bf16[1,1024,512]{2,1,0:T(8,128)(2,1)} copy(bf16[1,1024,512]{2,1,0:T(8,128)(2,1)} %bitcast.11) | data formatting | bytes 2097152
  83.5 0.0 copy-done
  83.5 1.0 %copy.15 = bf16[1,512,1024]{2,1,0:T(8,128)(2,1)} copy(bf16[1,512,1024]{2,1,0:T(8,128)(2,1)S(1)} %bitcast.10) | data formatting | bytes 2097152
  (1 shorter events, 0.0 us)
Async XLA Ops:
  0.6 0.7 copy-start.2
  78.2 0.7 copy-start.1
  81.1 2.4 %copy-start = (bf16[512,1024]{1,0:T(8,128)(2,1)S(1)}, bf16[512,1024]{1,0:T(8,128)(2,1)}, u32[]{:S(2)}) copy-start(bf16[512,1024]{1,0:T(8,128)(2,1)} %get-tuple-element.11) | copy-start | bytes 3145732

commit v2 on v1

--- a/solution.py
+++ b/solution.py
@@ -89,8 +89,9 @@
 
     ids0 = ids_ref[0:1, :]
     ids1 = ids_ref[1:2, :]
-    p0 = gate_ref[0:1, :]
-    p1 = gate_ref[1:2, :]
+    both = gate_ref[...].astype(F32)
+    p0 = both[0:1, :]
+    p1 = both[1:2, :]
     e_rows = hit_s.shape[0]
     e_iota = lax.broadcasted_iota(jnp.int32, (e_rows, tok_count), 0)
     hit = jnp.where(e_iota == ids0, 1.0, 0.0) + jnp.where(e_iota == ids1, 1.0, 0.0)
@@ -140,15 +141,27 @@
     def start_send(s):
         for k in range(2):
             send[k, pl.ds(pl.multiple_of(s * cap, 16), cap), :] = fill(s, k)
-            z_copy(s, k).start()
+            if unroll and 2 * (s - 1) + k < ahead:
+                z_copy(s, k).start()
+            elif not unroll:
+                pl.when(2 * (s - 1) + k < ahead)(lambda: z_copy(s, k).start())
 
     def spread(s, k):
         for i in range(1, nx):
             x_copy(s, k, i).start()
         f_copy(s, k, 0, c).start()
 
+    def kick(s, k):
+        z_copy(s, k).wait_send()
+        later = s + (k + ahead) // 2
+        if unroll and later < n_exp:
+            z_copy(later, (k + ahead) % 2).start()
+        elif not unroll:
+            pl.when(later < n_exp)(lambda: z_copy(later, (k + ahead) % 2).start())
+
     def f1(s):
         for k in range(2):
+            kick(s, k)
             z_copy(s, k).wait_recv()
             spread(s, k)
 
@@ -227,7 +240,8 @@
         return rcopy(g_out.at[s], g_back.at[s], ks.at[s], kr.at[s], exp_dev(down(s)))
 
     g_part[...] = jnp.zeros_like(g_part)
-    unroll = n_exp <= 4
+    unroll = n_exp == 4
+    ahead = 1
 
     def over(low, high, body):
         if unroll:
@@ -243,33 +257,40 @@
     cw_in.wait()
     cw_out.wait()
 
-    f1(1)
-    f2(0)
-    compute(0)
-    f1(2)
-    f2(1)
-    compute(1)
-    r1(0)
-
-    def steady(t):
-        f1(t)
-        f2(t - 1)
-        compute(t - 1)
-        r1(t - 2)
-
-        if unroll and t == 3:
-            back[0:cap, :] = r2(0)
-        else:
-            r2_send(t - 3)
-
     if unroll:
-        over(3, n_exp, steady)
+        f1(1)
+        f2(0)
+        f1(2)
+        f2(1)
+        compute(0)
+        f1(3)
+        f2(2)
+        compute(1)
+        r1(0)
+        compute(2)
+        r1(1)
+        back[0:cap, :] = r2(0)
     else:
+        f1(1)
+        f2(0)
+        compute(0)
+        f1(2)
+        f2(1)
+        compute(1)
+        r1(0)
         f1(3)
         f2(2)
         compute(2)
         r1(1)
         back[0:cap, :] = r2(0)
+
+        def steady(t):
+            f1(t)
+            f2(t - 1)
+            compute(t - 1)
+            r1(t - 2)
+            r2_send(t - 3)
+
         over(4, n_exp, steady)
     last = n_exp - 1
     f2(last)
@@ -311,8 +332,8 @@
         value = dot(hi, mine, 1, 0) + dot(lo, mine, 1, 0)
         gate0 += jnp.where(ids0 == up(s), value, 0.0)
         gate1 += jnp.where(ids1 == up(s), value, 0.0)
-    ggate_ref[0:8, :] = gate0 / p0
-    ggate_ref[8:16, :] = gate1 / p1
+    first = lax.broadcasted_iota(jnp.int32, (2, tok_count), 0) == 0
+    ggate_ref[...] = jnp.where(first, gate0[0:2] / p0, gate1[0:2] / p1).astype(BF16)
 
     over(1, n_exp, lambda s: b_copy(s).wait_recv())
     total = jnp.zeros((tok_count, width), F32)
@@ -323,8 +344,6 @@
     gtok_ref[...] = total.astype(BF16)
 
     def drain(s):
-        for k in range(2):
-            z_copy(s, k).wait_send()
         b_copy(s).wait_send()
         k_copy(s).wait_send()
 
@@ -357,14 +376,14 @@
     lanes = 128
     e_rows = (n_exp + 15) // 16 * 16
     vmem = pl.BlockSpec(memory_space=pltpu.VMEM)
-    hbm = pl.BlockSpec(memory_space=pl.ANY)
+    hbm = pl.BlockSpec(memory_space=pltpu.HBM)
     dma = pltpu.SemaphoreType.DMA
     far = max(nx - 1, 1)
     grad_tokens, gate_rows, grad_in, grad_out = pl.pallas_call(
         functools.partial(kernel, n_exp, n_dp, cap, width, hid),
         out_shape=(
             jax.ShapeDtypeStruct((tok_count, width), BF16),
-            jax.ShapeDtypeStruct((16, tok_count), F32),
+            jax.ShapeDtypeStruct((2, tok_count), BF16),
             jax.ShapeDtypeStruct((width, hid), BF16),
             jax.ShapeDtypeStruct((hid, width), BF16),
         ),
@@ -402,13 +421,12 @@
             dma((n_exp,)), dma((n_exp,)),
         ],
         compiler_params=pltpu.CompilerParams(
-            collective_id=0, has_side_effects=True, vmem_limit_bytes=60 * 1024 * 1024
+            collective_id=0, has_side_effects=True, vmem_limit_bytes=(30 if n_exp <= 4 else 56) * 1024 * 1024
         ),
     )(
-        expert_ids.T, gates.T.astype(F32), tokens, cotangent, expert_in[0], expert_out[0]
+        expert_ids.T, gates.T, tokens, cotangent, expert_in[0], expert_out[0]
     )
-    grad_gates = gate_rows[0::8].T.astype(BF16)
-    return grad_tokens, grad_gates, grad_in[None], grad_out[None]
+    return grad_tokens, gate_rows.T, grad_in[None], grad_out[None]
 
 
 def solution(mesh):

time: 84.7 us -> 76.6 us (0.904)
  Pallas kernels: 76.3 us -> 67 us
  local copies, waits for them, and re-layouts: 6.86 us -> 8.17 us
    pallas_call x1, Pallas kernels: 76.3 us -> 67 us  [per_device(): pl.pallas_call(functools.partial(kernel, n_exp, n_dp, cap, width, hid), o...]
    unnamed x9 -> x16, local copies, waits for them, and re-layouts: 6.33 us -> 8.17 us
where the time goes in v2:
time: 76.6 us; the launch traced here: 75.8 us
  Pallas kernels  67 us (87%)
  local copies, waits for them, and re-layouts  8.17 us (11%)
    pallas_call x1, Pallas kernels, per_device(): pl.pallas_call(functools.partial(kernel, n_exp, n_dp, cap, width, hid), o...  67 us
    unnamed x16, local copies, waits for them, and re-layouts  8.17 us

profile of v2, /device:TPU:0, one launch (start us, length us, event | category | flops | bytes accessed | tf_op | source)
XLA Modules:
  0.0 75.8 jit_solution(6107466200245080427)
XLA Ops:
  0.6 0.0 copy-start.4
  0.6 0.0 copy-start.5
  0.7 0.7 copy-done.4
  1.3 0.0 copy-done.5
  1.3 0.0 copy-start
  1.3 1.2 %copy-done = bf16[1,1024,512]{2,1,0:T(8,128)(2,1)S(1)} copy-done((bf16[1,1024,512]{2,1,0:T(8,128)(2,1)S(1)}, bf16[1,1024,512]{2,1,0:T(8,128)(2,1)}, u32[]{:S(2)}) %copy-start) | copy-done | bytes 1048600
  2.5 0.0 copy-start.1
  2.5 1.2 %copy-done.1 = bf16[1,512,1024]{2,1,0:T(8,128)(2,1)S(1)} copy-done((bf16[1,512,1024]{2,1,0:T(8,128)(2,1)S(1)}, bf16[1,512,1024]{2,1,0:T(8,128)(2,1)}, u32[]{:S(2)}) %copy-start.1) | copy-done | bytes 1048600
  3.8 0.0 copy-start.2
  3.8 0.9 %copy-done.2 = bf16[128,1024]{1,0:T(8,128)(2,1)S(1)} copy-done((bf16[128,1024]{1,0:T(8,128)(2,1)S(1)}, bf16[128,1024]{1,0:T(8,128)(2,1)}, u32[]{:S(2)}) %copy-start.2) | copy-done | bytes 262168
  4.7 0.0 copy-start.3
  4.7 0.9 %copy-done.3 = bf16[128,1024]{1,0:T(8,128)(2,1)S(1)} copy-done((bf16[128,1024]{1,0:T(8,128)(2,1)S(1)}, bf16[128,1024]{1,0:T(8,128)(2,1)}, u32[]{:S(2)}) %copy-start.3) | copy-done | bytes 262168
  5.7 67.0 %shard_map.93 = (bf16[128,1024]{1,0:T(8,128)(2,1)S(1)}, bf16[2,128]{1,0:T(2,128)(2,1)S(1)}, bf16[1024,512]{1,0:T(8,128)(2,1)S(1)}, bf16[512,1024]{1,0:T(8,128)(2,1)S(1)}) custom-call(s32[2,128]{1,0:T(2,128)S(1)} %bitcast.11, bf16[2,128]{1,0:T(2,128)(2,1)S(1)} %bitcast.12, bf16[128,1024]{1,0:T(8,128)(2,1)S(1)} %copy-done.2, bf16[128,1024]{1,0:T(8,128)(2,1)S(1)} %copy-done.3, ...), custom_call_target="tpu_custom_call" | custom-call | tf_op jit(solution)/shard_map/pallas_call | solution.py:382
  72.7 0.7 copy.14
  73.4 0.5 copy.15
  73.9 1.0 %copy.16 = bf16[1,1024,512]{2,1,0:T(8,128)(2,1)} copy(bf16[1,1024,512]{2,1,0:T(8,128)(2,1)S(1)} %bitcast.10) | data formatting | bytes 2097152
  74.8 1.0 %copy.17 = bf16[1,512,1024]{2,1,0:T(8,128)(2,1)} copy(bf16[1,512,1024]{2,1,0:T(8,128)(2,1)S(1)} %bitcast.9) | data formatting | bytes 2097152
Async XLA Ops:
  0.6 0.7 copy-start.4
  0.6 0.7 copy-start.5
  1.3 1.2 %copy-start = (bf16[1,1024,512]{2,1,0:T(8,128)(2,1)S(1)}, bf16[1,1024,512]{2,1,0:T(8,128)(2,1)}, u32[]{:S(2)}) copy-start(bf16[1,1024,512]{2,1,0:T(8,128)(2,1)} %param.10) | copy-start | bytes 3145732
  2.5 1.2 %copy-start.1 = (bf16[1,512,1024]{2,1,0:T(8,128)(2,1)S(1)}, bf16[1,512,1024]{2,1,0:T(8,128)(2,1)}, u32[]{:S(2)}) copy-start(bf16[1,512,1024]{2,1,0:T(8,128)(2,1)} %param.11) | copy-start | bytes 3145732
  3.8 0.9 %copy-start.2 = (bf16[128,1024]{1,0:T(8,128)(2,1)S(1)}, bf16[128,1024]{1,0:T(8,128)(2,1)}, u32[]{:S(2)}) copy-start(bf16[128,1024]{1,0:T(8,128)(2,1)} %tok_ref.1) | copy-start | bytes 786436
  4.7 0.9 %copy-start.3 = (bf16[128,1024]{1,0:T(8,128)(2,1)S(1)}, bf16[128,1024]{1,0:T(8,128)(2,1)}, u32[]{:S(2)}) copy-start(bf16[128,1024]{1,0:T(8,128)(2,1)} %cot_ref.1) | copy-start | bytes 786436

commit v3 on v2

--- a/solution.py
+++ b/solution.py
@@ -250,10 +250,11 @@
         else:
             lax.fori_loop(low, high, lambda s, t: (body(s), t)[1], 0)
 
+    start_send(1)
     for k in range(2):
         buf[k, rows(0, d), :] = fill(0, k)
         spread(0, k)
-    over(1, n_exp, start_send)
+    over(2, n_exp, start_send)
     cw_in.wait()
     cw_out.wait()
 
@@ -421,7 +422,7 @@
             dma((n_exp,)), dma((n_exp,)),
         ],
         compiler_params=pltpu.CompilerParams(
-            collective_id=0, has_side_effects=True, vmem_limit_bytes=(30 if n_exp <= 4 else 56) * 1024 * 1024
+            collective_id=0, has_side_effects=True, vmem_limit_bytes=58 * 1024 * 1024
         ),
     )(
         expert_ids.T, gates.T, tokens, cotangent, expert_in[0], expert_out[0]

time: 76.6 us -> 75.8 us (0.990)
  local copies, waits for them, and re-layouts: 8.17 us -> 5.51 us
  Pallas kernels: 67 us -> 68.9 us
    unnamed x16 -> x8, local copies, waits for them, and re-layouts: 8.17 us -> 5.51 us
    pallas_call x1, Pallas kernels: 67 us -> 68.9 us  [per_device(): pl.pallas_call(functools.partial(kernel, n_exp, n_dp, cap, width, hid), o...]
where the time goes in v3:
time: 75.8 us; the launch traced here: 75.1 us
  Pallas kernels  68.9 us (91%)
  local copies, waits for them, and re-layouts  5.51 us (7%)
    pallas_call x1, Pallas kernels, per_device(): pl.pallas_call(functools.partial(kernel, n_exp, n_dp, cap, width, hid), o...  68.9 us
    unnamed x8, local copies, waits for them, and re-layouts  5.51 us

profile of v3, /device:TPU:0, one launch (start us, length us, event | category | flops | bytes accessed | tf_op | source)
XLA Modules:
  0.0 75.1 jit_solution(16552369518244342214)
XLA Ops:
  0.6 68.9 %shard_map.93 = (bf16[128,1024]{1,0:T(8,128)(2,1)}, bf16[2,128]{1,0:T(2,128)(2,1)}, bf16[1024,512]{1,0:T(8,128)(2,1)}, bf16[512,1024]{1,0:T(8,128)(2,1)}) custom-call(s32[2,128]{1,0:T(2,128)} %bitcast.11, bf16[2,128]{1,0:T(2,128)(2,1)} %bitcast.12, bf16[128,1024]{1,0:T(8,128)(2,1)} %tok_ref.1, bf16[128,1024]{1,0:T(8,128)(2,1)} %cot_ref.1, ...), custom_call_target="tpu_custom_call" | custom-call | tf_op jit(solution)/shard_map/pallas_call | solution.py:383
  69.5 0.0 copy-start.1
  69.5 1.7 %copy.14 = bf16[128,1024]{1,0:T(8,128)(2,1)} copy(bf16[128,1024]{1,0:T(8,128)(2,1)} %get-tuple-element.16) | data formatting | bytes 524288
  71.2 0.0 copy-done.1
  71.2 0.5 copy.15
  71.7 0.0 copy-start
  71.7 2.4 %copy.16 = bf16[1,1024,512]{2,1,0:T(8,128)(2,1)} copy(bf16[1,1024,512]{2,1,0:T(8,128)(2,1)} %bitcast.10) | data formatting | bytes 2097152
  74.1 0.0 copy-done
  74.1 1.0 %copy.17 = bf16[1,512,1024]{2,1,0:T(8,128)(2,1)} copy(bf16[1,512,1024]{2,1,0:T(8,128)(2,1)S(1)} %bitcast.9) | data formatting | bytes 2097152
Async XLA Ops:
  69.5 1.7 %copy-start.1 = (bf16[2,128]{1,0:T(2,128)(2,1)S(1)}, bf16[2,128]{1,0:T(2,128)(2,1)}, u32[]{:S(2)}) copy-start(bf16[2,128]{1,0:T(2,128)(2,1)} %get-tuple-element.9) | copy-start | bytes 1540
  71.7 2.4 %copy-start = (bf16[512,1024]{1,0:T(8,128)(2,1)S(1)}, bf16[512,1024]{1,0:T(8,128)(2,1)}, u32[]{:S(2)}) copy-start(bf16[512,1024]{1,0:T(8,128)(2,1)} %get-tuple-element.11) | copy-start | bytes 3145732
